TPU v7x, 32 devices: a whole 2x2x4 slice. The times are simulated.
32 devices in a mesh: groups: 2 (over x), space: 16 (over z, y, core).
Axes of the slice: x: 2, y: 2, z: 4, core: 2. Of those that a mesh axis runs over, the one named last changes fastest.
Arguments:
- features: bfloat16 [4, 16, 8, 512], P('groups', 'space'), parts along dimension 0, may hold values from -60 to 60, as said below
- norm_gain: float32 [512], replicated, may hold values from 0.5 to 1.5
- norm_bias: float32 [512], replicated, may hold values from -3 to 3
- query_weight: bfloat16 [512, 512], replicated, may hold values from -1 to 1
- query_bias: float32 [512], replicated, may hold values from -3 to 3
- key_weight: bfloat16 [512, 512], replicated, may hold values from -3 to 3
- value_weight: bfloat16 [512, 512], replicated, may hold values from -0.25 to 0.25
- value_bias: float32 [512], replicated, may hold values from -3 to 3
- out_weight: bfloat16 [512, 512], replicated, may hold values from -0.25 to 0.25
- out_bias: float32 [512], replicated, may hold values from -3 to 3
- conv_weight: bfloat16 [3, 3, 3, 512, 512], P(None, None, None, None, 'space'), may hold values from -0.0546875 to 0.0546875
- conv_bias: float32 [512], replicated, may hold values from -3 to 3
Outputs:
- decoded: bfloat16 [6, 32, 16, 512], P('groups', 'space'), parts along dimension 0
There are 2 independent parts, one for each index of `groups`. A program takes and returns all parts, laid end to end along the dimension named above; an argument that names none is the same for every part. Nothing has to cross between parts.
Inputs may be any that keep to these rules, and one draw needn't show every extreme that they name: mid-block features of one video.
All inputs are finite; a program needn't handle non-finite values.
Results may differ from a plain program's by a relative error of at most 0.0079.
Values may be sent and summed in bfloat16 or wider, within the bound.
A program may use at most 128 MiB of HBM per device.

v0:
```python
import jax
import jax.numpy as jnp
from jax import lax
from jax.sharding import PartitionSpec as P

GROUPS = 32


EPSILON = 1e-06
NEGATIVE = -1e30


def with_halo(value, sides, width):
    for axis, dim in sides:
        count, length = (lax.axis_size(axis), value.shape[dim])
        up = [(i, (i + 1) % count) for i in range(count - 1)]
        down = [(j, i) for i, j in up]
        last = lax.slice_in_dim(value, length - width, length, axis=dim)
        leading = lax.slice_in_dim(value, 0, width, axis=dim)
        before = lax.ppermute(last, axis, up)
        after = lax.ppermute(leading, axis, down)
        value = jnp.concatenate([before, value, after], axis=dim)
    return value


def upsample_conv(row_band, weight):
    repeated = jnp.repeat(row_band[1:], 2, axis=0)
    frames = jnp.concatenate([row_band[:1], repeated], axis=0)
    doubled_rows = jnp.repeat(frames, 2, axis=1)[:, 1:-1]
    columns = jnp.repeat(doubled_rows, 2, axis=2)
    columns = jnp.concatenate([columns[:, :, :1], columns, columns[:, :, -1:]], axis=2)
    padded = jnp.concatenate([columns[:1], columns[:1], columns], axis=0)
    out_frames = frames.shape[0]
    out_rows = doubled_rows.shape[1] - 2
    out_cols = columns.shape[2] - 2
    channels = row_band.shape[3]
    out_width = weight.shape[4]
    result = jnp.zeros((out_frames * out_rows * out_cols, out_width), jnp.float32)
    for time_tap in range(3):
        for row_tap in range(3):
            for col_tap in range(3):
                window = padded[
                    time_tap : time_tap + out_frames,
                    row_tap : row_tap + out_rows,
                    col_tap : col_tap + out_cols,
                ]
                result = result + jnp.dot(
                    window.reshape(-1, channels),
                    weight[time_tap, row_tap, col_tap],
                    preferred_element_type=jnp.float32,
                )
    return result.reshape(out_frames, out_rows, out_cols, out_width)


def per_device(
    features,
    norm_gain,
    norm_bias,
    query_weight,
    query_bias,
    key_weight,
    value_weight,
    value_bias,
    out_weight,
    out_bias,
    conv_weight,
    conv_bias,
):
    frames, local_rows, columns, channels = features.shape
    spread = lax.axis_size("space")
    grouped = features.astype(jnp.float32).reshape(-1, GROUPS, channels // GROUPS)
    entries = grouped.shape[0] * grouped.shape[2] * spread
    group_mean = lax.psum(jnp.sum(grouped, axis=(0, 2)), "space") / entries
    centred = grouped - group_mean[None, :, None]
    variance = lax.psum(jnp.sum(centred * centred, axis=(0, 2)), "space") / entries
    normed = (
        (centred * lax.rsqrt(variance + EPSILON)[None, :, None]).reshape(-1, channels) * norm_gain
        + norm_bias
    ).astype(jnp.bfloat16)
    softmax_scale = channels ** (-0.5)
    queries = (
        (jnp.dot(normed, query_weight, preferred_element_type=jnp.float32) + query_bias)
        * softmax_scale
    ).astype(jnp.bfloat16)
    key_tiles = (
        jnp.dot(normed, key_weight, preferred_element_type=jnp.float32)
        .astype(jnp.bfloat16)
        .reshape(frames, local_rows, columns, channels)
    )
    value_tiles = (
        (jnp.dot(normed, value_weight, preferred_element_type=jnp.float32) + value_bias)
        .astype(jnp.bfloat16)
        .reshape(frames, local_rows, columns, channels)
    )
    local_count = queries.shape[0]
    query_frame = jnp.arange(local_count) // (local_rows * columns)
    running_max = jnp.full((local_count,), NEGATIVE, jnp.float32)
    key_piece = lax.all_gather(key_tiles, "space", axis=1, tiled=True)
    value_piece = lax.all_gather(value_tiles, "space", axis=1, tiled=True)
    per_frame = key_piece.shape[1] * key_piece.shape[2]
    key_rows = key_piece.reshape(-1, channels)
    value_rows = value_piece.reshape(-1, channels)
    key_frame = jnp.arange(key_rows.shape[0]) // per_frame
    allowed = query_frame[:, None] >= key_frame[None, :]
    scores = jnp.where(
        allowed, jnp.dot(queries, key_rows.T, preferred_element_type=jnp.float32), NEGATIVE
    )
    new_max = jnp.maximum(running_max, jnp.max(scores, axis=1))
    weights = jnp.where(allowed, jnp.exp(scores - new_max[:, None]), 0.0)
    denominator = jnp.sum(weights, axis=1)
    weighted = jnp.dot(weights.astype(jnp.bfloat16), value_rows, preferred_element_type=jnp.float32)
    running_max, denominator, weighted = (new_max, denominator, weighted)
    attended = (weighted / denominator[:, None]).astype(jnp.bfloat16)
    mixed_tokens = (
        features.reshape(-1, channels).astype(jnp.float32)
        + jnp.dot(attended, out_weight, preferred_element_type=jnp.float32)
        + out_bias
    ).astype(jnp.bfloat16)
    mixed_tokens = mixed_tokens.reshape(frames, local_rows, columns, channels)
    rimmed = with_halo(mixed_tokens, (("space", 1),), 1)
    position = lax.axis_index("space")
    upper_rim = jnp.where(position == 0, mixed_tokens, rimmed[:, :1])
    lower_rim = jnp.where(position == spread - 1, mixed_tokens, rimmed[:, -1:])
    row_band = jnp.concatenate([upper_rim, mixed_tokens, lower_rim], axis=1)
    convolved = upsample_conv(row_band, lax.all_gather(conv_weight, "space", axis=4, tiled=True))
    decoded = (convolved + conv_bias).astype(jnp.bfloat16)
    return decoded


def solution(mesh):
    placed = (
        P("groups", "space", None, None),
        P(),
        P(),
        P(),
        P(),
        P(),
        P(),
        P(),
        P(),
        P(),
        P(None, None, None, None, "space"),
        P(),
    )
    return jax.shard_map(
        per_device,
        mesh=mesh,
        in_specs=placed,
        out_specs=P("groups", "space", None, None),
        check_vma=False,
    )
```

profile of v0, /device:TPU:0, one launch (start us, length us, event | category | flops | bytes accessed | tf_op | source)
XLA Modules:
  0.0 172.2 jit_solution(1226590587753223035)
XLA Ops:
  8.2 36.0 %psum.14 = f32[32]{0:T(128)S(1)} all-reduce(f32[32]{0:T(128)S(1)} %reduce_sum.36), channel_id=1, replica_groups=mesh['groups'=2,'space'=16] {'space'}, use_global_device_ids=true, to_apply=%region_2.0 | all-reduce | flops 32 | bytes 256 | tf_op jit(solution)/shard_map/psum | solution.py:73
  45.3 30.6 %psum.15 = f32[32]{0:T(128)S(1)} all-reduce(f32[32]{0:T(128)S(1)} %reduce_sum.46), channel_id=1, replica_groups=mesh['groups'=2,'space'=16] {'space'}, use_global_device_ids=true, to_apply=%region_5.6 | all-reduce | flops 32 | bytes 256 | tf_op jit(solution)/shard_map/psum | solution.py:75
  77.0 19.4 %all_gather.9 = bf16[2,16,8,512]{3,2,1,0:T(8,128)(2,1)S(1)} all-gather(bf16[2,1,8,512]{3,2,1,0:T(8,128)(2,1)S(1)} %fusion.6), channel_id=1, replica_groups=mesh['groups'=2,'space'=16] {'space'}, dimensions={1}, use_global_device_ids=true | all-gather | bytes 278528 | tf_op jit(solution)/shard_map/all_gather | solution.py:98
  96.4 1.5 fusion.46
  99.3 21.3 %all_gather.10 = bf16[2,16,8,512]{3,2,1,0:T(8,128)(2,1)S(1)} all-gather(bf16[2,1,8,512]{3,2,1,0:T(8,128)(2,1)S(1)} %fusion.8), channel_id=1, replica_groups=mesh['groups'=2,'space'=16] {'space'}, dimensions={1}, use_global_device_ids=true | all-gather | bytes 278528 | tf_op jit(solution)/shard_map/all_gather | solution.py:99
  120.5 1.4 fusion.7
  121.9 2.2 %collective-permute-start = (bf16[2,1,8,512]{3,2,0,1:T(8,128)(2,1)S(1)}, bf16[2,1,8,512]{3,2,0,1:T(8,128)(2,1)S(1)}, u32[]{:S(2)}, u32[]{:S(2)}) collective-permute-start(bf16[2,1,8,512]{3,2,0,1:T(8,128)(2,1)S(1)} %fusion.7), channel_id=1, source_target_pairs={{0,1},{1,2},{2,3},{3,4},{4,5},{5,6},{6,7},{7,8},{8,9},{9,10},{10,1... | collective-permute-start | bytes 49160 | tf_op jit(solution)/shard_map/ppermute | solution.py:20
  125.5 1.8 %collective-permute-done.1 = bf16[2,1,8,512]{3,2,0,1:T(8,128)(2,1)S(1)} collective-permute-done((bf16[2,1,8,512]{3,2,0,1:T(8,128)(2,1)S(1)}, bf16[2,1,8,512]{3,2,0,1:T(8,128)(2,1)S(1)}, u32[]{:S(2)}, u32[]{:S(2)}) %collective-permute-start.1) | collective-permute-done | bytes 16416 | tf_op jit(solution)/shard_map/ppermute | solution.py:21
  129.8 1.3 convolution_add_fusion.25
  131.2 1.3 convolution_add_fusion.24
  132.5 1.3 convolution_add_fusion.23
  135.2 1.3 convolution_add_fusion.21
  137.9 1.3 convolution_add_fusion.19
  139.2 1.3 convolution_add_fusion.18
  141.9 1.3 convolution_add_fusion.16
  143.2 1.3 convolution_add_fusion.15
  145.9 1.3 convolution_add_fusion.13
  148.6 1.3 convolution_add_fusion.11
  149.9 1.3 convolution_add_fusion.10
  152.6 1.3 convolution_add_fusion.8
  153.9 1.3 convolution_add_fusion.7
  156.6 1.3 convolution_add_fusion.5
  158.0 1.3 convolution_add_fusion.4
  160.6 1.3 convolution_add_fusion.2
  (55 shorter events, 23.0 us)
Async XLA Ops:
  6.5 69.6 %copy-start = (bf16[512,512]{1,0:T(8,128)(2,1)S(1)}, bf16[512,512]{1,0:T(8,128)(2,1)}, u32[]{:S(2)}) copy-start(bf16[512,512]{1,0:T(8,128)(2,1)} %param.17) | copy-start | bytes 1572868
  6.5 122.0 %all-gather.2.cloned.1.call-start = ((), (), s32[]{:S(2)}) async-start(), calls=%async_computation | async-start | bytes 15040512 | tf_op jit(solution)/shard_map/all_gather | solution.py:125
  121.9 3.6 %collective-permute-start = (bf16[2,1,8,512]{3,2,0,1:T(8,128)(2,1)S(1)}, bf16[2,1,8,512]{3,2,0,1:T(8,128)(2,1)S(1)}, u32[]{:S(2)}, u32[]{:S(2)}) collective-permute-start(bf16[2,1,8,512]{3,2,0,1:T(8,128)(2,1)S(1)} %fusion.7), channel_id=1, source_target_pairs={{0,1},{1,2},{2,3},{3,4},{4,5},{5,6},{6,7},{7,8},{8,9},{9,10},{10,1... | collective-permute-start | bytes 49160 | tf_op jit(solution)/shard_map/ppermute | solution.py:20
  124.2 3.1 %collective-permute-start.1 = (bf16[2,1,8,512]{3,2,0,1:T(8,128)(2,1)S(1)}, bf16[2,1,8,512]{3,2,0,1:T(8,128)(2,1)S(1)}, u32[]{:S(2)}, u32[]{:S(2)}) collective-permute-start(bf16[2,1,8,512]{3,2,0,1:T(8,128)(2,1)S(1)} %fusion.7), channel_id=1, source_target_pairs={{1,0},{2,1},{3,2},{4,3},{5,4},{6,5},{7,6},{8,7},{9,8},{10,9},{11,1... | collective-permute-start | bytes 49160 | tf_op jit(solution)/shard_map/ppermute | solution.py:21
  128.3 36.3 %copy-start.1 = (f32[512]{0:T(512)S(1)}, f32[512]{0:T(512)}, u32[]{:S(2)}) copy-start(f32[512]{0:T(512)} %param.23) | copy-start | bytes 6148
Sparse Core Ops, SparseCore 0:
  9.6 116.6 all-gather.1
where the time goes:
time: 175 us; the launch traced here: 172 us
  blocking collectives  107 us (61%)
  matrix products  41 us (23%)
  between operations  13.8 us (8%)
  starting transfers between devices  3.54 us (2%)
  other arithmetic  3.15 us (2%)
  waiting for transfers between devices  2.49 us (1%)
    psum x1, blocking collectives, per_device(): group_mean = lax.psum(jnp.sum(grouped, axis=(0, 2)), 'space') / entries  36 us
    dot_general x27, matrix products, upsample_conv(): jnp.dot(window.reshape(-1, channels), weight[time_tap, row_tap, col_tap],...  35.9 us
    psum x1, blocking collectives, per_device(): lax.psum(jnp.sum(centred * centred, axis=(0, 2)), 'space') / entries  30.6 us
    all_gather x1, blocking collectives, per_device(): value_piece = lax.all_gather(value_tiles, 'space', axis=1, tiled=True)  21.3 us
    all_gather x1, blocking collectives, per_device(): key_piece = lax.all_gather(key_tiles, 'space', axis=1, tiled=True)  19.4 us
  transfers between devices with their start and end apart: 3, of which 1 were waited for; matrix products, arithmetic and copies ran while one was open for 5% of the time, Pallas kernels for 0%

commit v1 on v0

--- a/solution.py
+++ b/solution.py
@@ -1,6 +1,10 @@
+import functools
+
 import jax
 import jax.numpy as jnp
 from jax import lax
+from jax.experimental import pallas as pl
+from jax.experimental.pallas import tpu as pltpu
 from jax.sharding import PartitionSpec as P
 
 GROUPS = 32
@@ -52,7 +56,7 @@
     return result.reshape(out_frames, out_rows, out_cols, out_width)
 
 
-def per_device(
+def per_device_sharded(
     features,
     norm_gain,
     norm_bias,
@@ -127,6 +131,343 @@
     return decoded
 
 
+MESH = pl.DeviceIdType.MESH
+F32 = jnp.float32
+BF16 = jnp.bfloat16
+
+
+def dot_t(a, b):
+    return lax.dot_general(a, b, (((1,), (1,)), ((), ())), preferred_element_type=F32)
+
+
+def dot_n(a, b):
+    return jnp.dot(a, b, preferred_element_type=F32)
+
+
+def group_total(row, width):
+    channels = row.shape[1]
+    lane = lax.broadcasted_iota(jnp.int32, row.shape, 1)
+    step = 1
+    while step < width:
+        high = (lane // step) % 2 == 1
+        row = row + jnp.where(
+            high, pltpu.roll(row, step, 1), pltpu.roll(row, channels - step, 1)
+        )
+        step *= 2
+    return row
+
+
+def fold_conv_weights(conv_v, w0_ref, w1_ref):
+    outs, channels = conv_v.shape[1], conv_v.shape[2]
+    zero = jnp.zeros((outs, channels), BF16)
+    combos = (
+        (w0_ref, 0, (0, 1, 2)),
+        (w0_ref, 1, (0, 1)),
+        (w0_ref, 2, (0,)),
+        (w1_ref, 0, (2,)),
+        (w1_ref, 1, (1, 2)),
+    )
+    spatial = {
+        (0, 0): (0,),
+        (0, 1): (1, 2),
+        (1, 1): (0, 1),
+        (1, 2): (2,),
+    }
+    for ref, slot, times in combos:
+        summed = {}
+        for b in range(3):
+            for e in range(3):
+                value = conv_v[times[0] * 9 + b * 3 + e].astype(F32)
+                for a in times[1:]:
+                    value = value + conv_v[a * 9 + b * 3 + e].astype(F32)
+                summed[b, e] = value
+        for p in range(2):
+            for dr in range(3):
+                rows = spatial.get((p, dr))
+                if rows is not None:
+                    by_col = []
+                    for e in range(3):
+                        value = summed[rows[0], e]
+                        for b in rows[1:]:
+                            value = value + summed[b, e]
+                        by_col.append(value)
+                for q in range(2):
+                    for dc in range(3):
+                        cols = spatial.get((q, dc))
+                        if rows is None or cols is None:
+                            piece = zero
+                        else:
+                            value = by_col[cols[0]]
+                            for e in cols[1:]:
+                                value = value + by_col[e]
+                            piece = value.astype(BF16)
+                        at = slot * 4 * outs + (p * 2 + q) * outs
+                        tap = (dr * 3 + dc) * channels
+                        ref[at : at + outs, tap : tap + channels] = piece
+
+
+def shifted_inputs(frame, x_ref):
+    height, width, channels = frame.shape
+    column = lax.broadcasted_iota(jnp.int32, frame.shape, 1)
+    left = jnp.where(column == 0, frame, jnp.roll(frame, 1, axis=1))
+    right = jnp.where(column == width - 1, frame, jnp.roll(frame, -1, axis=1))
+    for dc, plane in enumerate((left, frame, right)):
+        up = jnp.concatenate([plane[:1], plane[:-1]], axis=0)
+        down = jnp.concatenate([plane[1:], plane[-1:]], axis=0)
+        for dr, moved in enumerate((up, plane, down)):
+            tap = (dr * 3 + dc) * channels
+            x_ref[:, tap : tap + channels] = moved.reshape(height * width, channels).astype(BF16)
+
+
+def fused_kernel(
+    count,
+    feat_ref,
+    gain_ref,
+    nbias_ref,
+    qw_ref,
+    qb_ref,
+    kw_ref,
+    vw_ref,
+    vb_ref,
+    ow_ref,
+    ob_ref,
+    cw_ref,
+    cb_ref,
+    out_ref,
+    gath,
+    qw,
+    kw,
+    vw,
+    ow,
+    cw,
+    w0_ref,
+    w1_ref,
+    x0_ref,
+    x1_ref,
+    sendbuf,
+    recvbuf,
+    wide,
+    load_sem,
+    fsend_sem,
+    frecv_sem,
+    osend_sem,
+    orecv_sem,
+):
+    me = lax.axis_index("space")
+    chips = count // 2
+    sibling = me + 1 - 2 * lax.rem(me, 2)
+    width, channels = feat_ref.shape[0] // 2, feat_ref.shape[1]
+
+    barrier = pltpu.get_barrier_semaphore()
+    for k in range(1, count):
+        pl.semaphore_signal(
+            barrier, inc=1, device_id={"space": lax.rem(me + k, count)}, device_id_type=MESH
+        )
+    loads = [
+        pltpu.make_async_copy(s, d, load_sem.at[i])
+        for i, (s, d) in enumerate(
+            ((feat_ref, gath.at[me]), (cw_ref, cw), (qw_ref, qw), (kw_ref, kw), (vw_ref, vw), (ow_ref, ow))
+        )
+    ]
+    for load in loads:
+        load.start()
+    pl.semaphore_wait(barrier, count - 1)
+
+    def feat_copy(src, block, to, slot):
+        return pltpu.make_async_remote_copy(
+            src_ref=src,
+            dst_ref=gath.at[block],
+            send_sem=fsend_sem.at[slot],
+            recv_sem=frecv_sem.at[block],
+            device_id={"space": to},
+            device_id_type=MESH,
+        )
+
+    sends = [
+        feat_copy(feat_ref, me, lax.rem(me + 2 * k, count), k) for k in range(1, chips)
+    ] + [feat_copy(feat_ref, me, sibling, 0)]
+    for send in sends:
+        send.start()
+
+    loads[1].wait()
+    fold_conv_weights(cw, w0_ref, w1_ref)
+
+    for k in range(1, chips):
+        block = lax.rem(me + count - 2 * k, count)
+        feat_copy(feat_ref, block, sibling, 0).wait_recv()
+        forward = feat_copy(gath.at[block], block, sibling, chips + k)
+        forward.start()
+        sends.append(forward)
+    loads[0].wait()
+    for k in range(chips):
+        block = lax.rem(sibling + count - 2 * k, count)
+        feat_copy(feat_ref, block, sibling, 0).wait_recv()
+
+    tokens = count * 2 * width
+    feats = gath[...].reshape(tokens, channels).astype(F32)
+    group_width = channels // GROUPS
+    entries = tokens * group_width
+    column = jnp.broadcast_to(jnp.sum(feats, axis=0, keepdims=True), (8, channels))
+    mean = group_total(column, group_width)[:1] / entries
+    centred = feats - mean
+    column = jnp.broadcast_to(jnp.sum(centred * centred, axis=0, keepdims=True), (8, channels))
+    variance = group_total(column, group_width)[:1] / entries
+    normed = (centred * lax.rsqrt(variance + EPSILON) * gain_ref[...] + nbias_ref[...]).astype(BF16)
+    for load in loads[2:]:
+        load.wait()
+    queries = ((dot_n(normed, qw[...]) + qb_ref[...]) * channels ** (-0.5)).astype(BF16)
+    keys = dot_n(normed, kw[...]).astype(BF16)
+    values = (dot_n(normed, vw[...]) + vb_ref[...]).astype(BF16)
+    scores = dot_t(queries, keys)
+    query_frame = (lax.broadcasted_iota(jnp.int32, scores.shape, 0) // width) % 2
+    key_frame = (lax.broadcasted_iota(jnp.int32, scores.shape, 1) // width) % 2
+    allowed = query_frame >= key_frame
+    scores = jnp.where(allowed, scores, NEGATIVE)
+    top = jnp.max(scores, axis=1, keepdims=True)
+    weights = jnp.where(allowed, jnp.exp(scores - top), 0.0)
+    denominator = jnp.sum(weights, axis=1, keepdims=True)
+    attended = (dot_n(weights.astype(BF16), values) / denominator).astype(BF16)
+    mixed = (
+        gath[...].reshape(tokens, channels).astype(F32) + dot_n(attended, ow[...]) + ob_ref[...]
+    )
+    mixed = mixed.astype(BF16).astype(F32).reshape(count, 2, width, channels)
+    shifted_inputs(mixed[:, 0], x0_ref)
+    shifted_inputs(mixed[:, 1], x1_ref)
+
+    outs = cw_ref.shape[1]
+    lanes = 4 * outs
+    bias_row = jnp.broadcast_to(cb_ref[...], (8, channels))
+    own = jnp.zeros((8, outs), F32)
+    for k in range(count):
+        own = jnp.where(me == k, bias_row[:, k * outs : (k + 1) * outs], own)
+    bias = jnp.concatenate([own] * 4, axis=1)[:1]
+    first = dot_t(x0_ref[...], w0_ref[...])
+    second = dot_t(x1_ref[...], w1_ref[...])
+    frames = [
+        first[:, :lanes] + bias,
+        first[:, lanes : 2 * lanes] + second[:, :lanes] + bias,
+        first[:, 2 * lanes :] + second[:, lanes:] + bias,
+    ]
+    frames = [f.reshape(count, width, lanes) for f in frames]
+    packed = jnp.concatenate(frames + [jnp.zeros_like(frames[0])], axis=1)
+    sendbuf[...] = packed.astype(BF16)
+
+    def out_copy(row, source, to, slot):
+        return pltpu.make_async_remote_copy(
+            src_ref=sendbuf.at[row],
+            dst_ref=recvbuf.at[source],
+            send_sem=osend_sem.at[slot],
+            recv_sem=orecv_sem.at[source],
+            device_id={"space": to},
+            device_id_type=MESH,
+        )
+
+    for k in range(1, count):
+        to = lax.rem(me + k, count)
+        send = out_copy(to, me, to, k)
+        send.start()
+        sends.append(send)
+    own_copy = pltpu.make_async_copy(sendbuf.at[me], recvbuf.at[me], osend_sem.at[0])
+    own_copy.start()
+    own_copy.wait()
+    for k in range(1, count):
+        source = lax.rem(me + count - k, count)
+        out_copy(source, source, me, k).wait_recv()
+
+    each = 128 // outs
+    for j in range(count // each):
+        parts = [recvbuf[j * each + i].astype(F32) for i in range(each)]
+        for p in range(2):
+            for q in range(2):
+                at = (p * 2 + q) * outs
+                joined = jnp.concatenate([part[:, at : at + outs] for part in parts], axis=1)
+                for t in range(3):
+                    base = (t * 2 + p) * 2 * width + q
+                    wide[j, pl.ds(base, width, stride=2), :] = joined[t * width : (t + 1) * width]
+    for j in range(count // each):
+        out_ref[:, j * 128 : (j + 1) * 128] = wide[j].astype(BF16)
+    for send in sends:
+        send.wait_send()
+
+
+def per_device_fused(
+    features,
+    norm_gain,
+    norm_bias,
+    query_weight,
+    query_bias,
+    key_weight,
+    value_weight,
+    value_bias,
+    out_weight,
+    out_bias,
+    conv_weight,
+    conv_bias,
+):
+    count = lax.axis_size("space")
+    frames, _, width, channels = features.shape
+    outs = conv_weight.shape[4]
+    rows = count * width
+    taps = jnp.swapaxes(conv_weight, 3, 4).reshape(27, outs, channels)
+    vmem = pl.BlockSpec(memory_space=pltpu.VMEM)
+    hbm = pl.BlockSpec(memory_space=pl.ANY)
+    square = pltpu.VMEM((channels, channels), BF16)
+    row = lambda v: v.reshape(1, channels)
+    out_rows = 3 * 2 * 2 * width
+    decoded = pl.pallas_call(
+        functools.partial(fused_kernel, count),
+        out_shape=jax.ShapeDtypeStruct((out_rows, channels), BF16),
+        in_specs=[hbm, vmem, vmem, hbm, vmem, hbm, hbm, vmem, hbm, vmem, hbm, vmem],
+        out_specs=vmem,
+        scratch_shapes=[
+            pltpu.VMEM((count, frames * width, channels), BF16),
+            square,
+            square,
+            square,
+            square,
+            pltpu.VMEM((27, outs, channels), BF16),
+            pltpu.VMEM((12 * outs, 9 * channels), BF16),
+            pltpu.VMEM((8 * outs, 9 * channels), BF16),
+            pltpu.VMEM((rows, 9 * channels), BF16),
+            pltpu.VMEM((rows, 9 * channels), BF16),
+            pltpu.VMEM((count, 4 * width, 4 * outs), BF16),
+            pltpu.VMEM((count, 4 * width, 4 * outs), BF16),
+            pltpu.VMEM((channels // 128, out_rows, 128), F32),
+            pltpu.SemaphoreType.DMA((6,)),
+            pltpu.SemaphoreType.DMA((count,)),
+            pltpu.SemaphoreType.DMA((count,)),
+            pltpu.SemaphoreType.DMA((count,)),
+            pltpu.SemaphoreType.DMA((count,)),
+        ],
+        compiler_params=pltpu.CompilerParams(
+            collective_id=0, has_side_effects=True, vmem_limit_bytes=44 * 1024 * 1024
+        ),
+    )(
+        features.reshape(frames * width, channels),
+        row(norm_gain),
+        row(norm_bias),
+        query_weight,
+        row(query_bias),
+        key_weight,
+        value_weight,
+        row(value_bias),
+        out_weight,
+        row(out_bias),
+        taps,
+        row(conv_bias),
+    )
+    return decoded.reshape(3, 2, 2 * width, channels)
+
+
+def per_device(features, *rest):
+    count = lax.axis_size("space")
+    frames, local_rows, width, channels = features.shape
+    outs = rest[9].shape[4]
+    if (frames, local_rows, width) == (2, 1, 8) and outs == 32 and count % 4 == 0:
+        return per_device_fused(features, *rest)
+    return per_device_sharded(features, *rest)
+
+
 def solution(mesh):
     placed = (
         P("groups", "space", None, None),

time: 175 us -> 29.2 us (0.17); the launches traced: 172 us -> 28.8 us
  blocking collectives: 107 us -> 0 us
  matrix products: 41 us -> 0 us
  Pallas kernels: 0 us -> 21.3 us
  between operations: 13.8 us -> 0.03 us
  local copies, waits for them, and re-layouts: 1.01 us -> 7.44 us
  starting transfers between devices: 3.54 us -> 0 us
  other arithmetic: 3.15 us -> 0 us
  waiting for transfers between devices: 2.49 us -> 0 us
    psum x2 -> x0, blocking collectives: 66.6 us -> none  [the longest x1 36 us: per_device(): group_mean = lax.psum(jnp.sum(grouped, axis=(0, 2)), 'space') / entries]
    dot_general x31 -> x0, matrix products: 41 us -> none  [the longest x27 35.9 us: upsample_conv(): jnp.dot(window.reshape(-1, channels), weight[time_tap, row_tap, col_tap],...]
    all_gather x2 -> x0, blocking collectives: 40.6 us -> none  [the longest x1 21.3 us: per_device(): value_piece = lax.all_gather(value_tiles, 'space', axis=1, tiled=True)]
    pallas_call x0 -> x1, Pallas kernels: none -> 21.3 us  [per_device_fused(): pl.pallas_call(functools.partial(fused_kernel, count), out_shape=jax.Shap...]
    unnamed x4 -> x25, local copies, waits for them, and re-layouts: 0.01 us -> 7.44 us
    ppermute x2 -> x0, starting transfers between devices: 3.54 us -> none  [the longest x1 2.25 us: with_halo(): before = lax.ppermute(last, axis, up)]
    reduce_sum x5 -> x0, other arithmetic: 1.9 us -> none  [the longest x2 0.86 us: per_device(): jnp.sum(centred * centred, axis=(0, 2))]
    ppermute x2 -> x0, waiting for transfers between devices: 1.76 us -> none  [the longest x1 1.76 us: with_halo(): after = lax.ppermute(leading, axis, down)]
  transfers between devices with their start and end apart: 3 -> 0, of which waited for: 1 -> 0; matrix products, arithmetic and copies ran while one was open for 5% -> 0% of each run, Pallas kernels for 0% -> 0%
where the time goes in v1:
time: 29.2 us; the launch traced here: 28.8 us
  Pallas kernels  21.3 us (73%)
  local copies, waits for them, and re-layouts  7.44 us (25%)
    pallas_call x1, Pallas kernels, per_device_fused(): pl.pallas_call(functools.partial(fused_kernel, count), out_shape=jax.Shap...  21.3 us
    unnamed x25, local copies, waits for them, and re-layouts  7.44 us

profile of v1, /device:TPU:0, one launch (start us, length us, event | category | flops | bytes accessed | tf_op | source)
XLA Modules:
  0.0 28.8 jit_solution(6745829958033626522)
XLA Ops:
  0.0 0.0 copy-start.11
  0.0 0.0 copy-start.10
  0.0 0.0 copy-start.9
  0.0 0.0 copy-start.8
  0.0 0.0 copy-start.7
  0.0 0.0 copy-start.6
  0.0 0.7 %copy-done.11 = f32[512]{0:T(512)S(1)} copy-done((f32[512]{0:T(512)S(1)}, f32[512]{0:T(512)}, u32[]{:S(2)}) %copy-start.11) | copy-done | bytes 2072
  0.7 0.0 copy-done.10
  0.7 0.0 copy-done.9
  0.7 0.0 copy-done.8
  0.7 0.0 copy-done.7
  0.7 0.0 copy-done.6
  0.8 0.0 copy-start
  0.8 1.2 %copy-done = bf16[3,3,3,512,32]{3,4,2,1,0:T(8,128)(2,1)S(1)} copy-done((bf16[3,3,3,512,32]{3,4,2,1,0:T(8,128)(2,1)S(1)}, bf16[3,3,3,512,32]{3,4,2,1,0:T(8,128)(2,1)}, u32[]{:S(2)}) %copy-start) | copy-done | bytes 884760
  1.9 1.0 %copy-done.1 = bf16[512,512]{1,0:T(8,128)(2,1)S(1)} copy-done((bf16[512,512]{1,0:T(8,128)(2,1)S(1)}, bf16[512,512]{1,0:T(8,128)(2,1)}, u32[]{:S(2)}) %copy-start.1) | copy-done | bytes 524312
  3.0 0.0 copy-start.2
  3.0 1.0 %copy-done.2 = bf16[512,512]{1,0:T(8,128)(2,1)S(1)} copy-done((bf16[512,512]{1,0:T(8,128)(2,1)S(1)}, bf16[512,512]{1,0:T(8,128)(2,1)}, u32[]{:S(2)}) %copy-start.2) | copy-done | bytes 524312
  4.0 0.0 copy-start.3
  4.0 1.0 %copy-done.3 = bf16[512,512]{1,0:T(8,128)(2,1)S(1)} copy-done((bf16[512,512]{1,0:T(8,128)(2,1)S(1)}, bf16[512,512]{1,0:T(8,128)(2,1)}, u32[]{:S(2)}) %copy-start.3) | copy-done | bytes 524312
  5.1 0.0 copy-start.4
  5.1 1.0 %copy-done.4 = bf16[512,512]{1,0:T(8,128)(2,1)S(1)} copy-done((bf16[512,512]{1,0:T(8,128)(2,1)S(1)}, bf16[512,512]{1,0:T(8,128)(2,1)}, u32[]{:S(2)}) %copy-start.4) | copy-done | bytes 524312
  6.1 0.7 %copy-done.5 = bf16[2,1,8,512]{3,2,1,0:T(8,128)(2,1)S(1)} copy-done((bf16[2,1,8,512]{3,2,1,0:T(8,128)(2,1)S(1)}, bf16[2,1,8,512]{3,2,1,0:T(8,128)(2,1)}, u32[]{:S(2)}) %copy-start.5) | copy-done | bytes 16408
  6.8 21.3 %shard_map.118 = bf16[96,512]{1,0:T(8,128)(2,1)S(1)} custom-call(bf16[16,512]{1,0:T(8,128)(2,1)S(1)} %bitcast.13, f32[1,512]{1,0:T(1,128)S(1)} %bitcast.14, f32[1,512]{1,0:T(1,128)S(1)} %bitcast.15, bf16[512,512]{1,0:T(8,128)(2,1)S(1)} %copy-done.1, f32[1,512]{1,0:T(1,128)S(1)} %bitcast.16, bf16[512,512]{1,0:T(8,128)(2,1)S(1)} %copy-done.2, ...), custom_call_target="tpu_custom_call" | custom-call | tf_op jit(solution)/shard_map/pallas_call | solution.py:417
  28.2 0.6 %copy.14 = bf16[3,2,16,512]{3,2,1,0:T(8,128)(2,1)} copy(bf16[3,2,16,512]{3,2,1,0:T(8,128)(2,1)S(1)} %bitcast.12) | data formatting | bytes 196608
  (2 shorter events, 0.0 us)
Async XLA Ops:
  0.0 0.7 %copy-start.11 = (f32[512]{0:T(512)S(1)}, f32[512]{0:T(512)}, u32[]{:S(2)}) copy-start(f32[512]{0:T(512)} %param.23) | copy-start | bytes 6148
  0.0 0.7 %copy-start.10 = (f32[512]{0:T(512)S(1)}, f32[512]{0:T(512)}, u32[]{:S(2)}) copy-start(f32[512]{0:T(512)} %param.21) | copy-start | bytes 6148
  0.0 0.7 %copy-start.9 = (f32[512]{0:T(512)S(1)}, f32[512]{0:T(512)}, u32[]{:S(2)}) copy-start(f32[512]{0:T(512)} %param.19) | copy-start | bytes 6148
  0.0 0.7 %copy-start.8 = (f32[512]{0:T(512)S(1)}, f32[512]{0:T(512)}, u32[]{:S(2)}) copy-start(f32[512]{0:T(512)} %param.16) | copy-start | bytes 6148
  0.0 0.7 %copy-start.7 = (f32[512]{0:T(512)S(1)}, f32[512]{0:T(512)}, u32[]{:S(2)}) copy-start(f32[512]{0:T(512)} %param.14) | copy-start | bytes 6148
  0.0 0.7 %copy-start.6 = (f32[512]{0:T(512)S(1)}, f32[512]{0:T(512)}, u32[]{:S(2)}) copy-start(f32[512]{0:T(512)} %param.13) | copy-start | bytes 6148
  0.8 1.2 %copy-start = (bf16[3,3,3,512,32]{3,4,2,1,0:T(8,128)(2,1)S(1)}, bf16[3,3,3,512,32]{3,4,2,1,0:T(8,128)(2,1)}, u32[]{:S(2)}) copy-start(bf16[3,3,3,512,32]{3,4,2,1,0:T(8,128)(2,1)} %param.22) | copy-start | bytes 2654212
  1.9 1.0 %copy-start.1 = (bf16[512,512]{1,0:T(8,128)(2,1)S(1)}, bf16[512,512]{1,0:T(8,128)(2,1)}, u32[]{:S(2)}) copy-start(bf16[512,512]{1,0:T(8,128)(2,1)} %qw_ref.1) | copy-start | bytes 1572868
  3.0 1.0 %copy-start.2 = (bf16[512,512]{1,0:T(8,128)(2,1)S(1)}, bf16[512,512]{1,0:T(8,128)(2,1)}, u32[]{:S(2)}) copy-start(bf16[512,512]{1,0:T(8,128)(2,1)} %kw_ref.1) | copy-start | bytes 1572868
  4.0 1.0 %copy-start.3 = (bf16[512,512]{1,0:T(8,128)(2,1)S(1)}, bf16[512,512]{1,0:T(8,128)(2,1)}, u32[]{:S(2)}) copy-start(bf16[512,512]{1,0:T(8,128)(2,1)} %vw_ref.1) | copy-start | bytes 1572868
  5.1 1.0 %copy-start.4 = (bf16[512,512]{1,0:T(8,128)(2,1)S(1)}, bf16[512,512]{1,0:T(8,128)(2,1)}, u32[]{:S(2)}) copy-start(bf16[512,512]{1,0:T(8,128)(2,1)} %ow_ref.1) | copy-start | bytes 1572868
  6.1 0.7 %copy-start.5 = (bf16[2,1,8,512]{3,2,1,0:T(8,128)(2,1)S(1)}, bf16[2,1,8,512]{3,2,1,0:T(8,128)(2,1)}, u32[]{:S(2)}) copy-start(bf16[2,1,8,512]{3,2,1,0:T(8,128)(2,1)} %param.12) | copy-start | bytes 49156

commit v2 on v1

--- a/solution.py
+++ b/solution.py
@@ -240,6 +240,12 @@
     vw,
     ow,
     cw,
+    gain,
+    nbias,
+    qb,
+    vb,
+    ob,
+    cb,
     w0_ref,
     w1_ref,
     x0_ref,
@@ -266,7 +272,20 @@
     loads = [
         pltpu.make_async_copy(s, d, load_sem.at[i])
         for i, (s, d) in enumerate(
-            ((feat_ref, gath.at[me]), (cw_ref, cw), (qw_ref, qw), (kw_ref, kw), (vw_ref, vw), (ow_ref, ow))
+            (
+                (feat_ref, gath.at[me]),
+                (cw_ref, cw),
+                (gain_ref, gain),
+                (nbias_ref, nbias),
+                (qw_ref, qw),
+                (kw_ref, kw),
+                (vw_ref, vw),
+                (ow_ref, ow),
+                (qb_ref, qb),
+                (vb_ref, vb),
+                (ob_ref, ob),
+                (cb_ref, cb),
+            )
         )
     ]
     for load in loads:
@@ -298,6 +317,8 @@
         forward = feat_copy(gath.at[block], block, sibling, chips + k)
         forward.start()
         sends.append(forward)
+    for load in loads[2:]:
+        load.wait()
     loads[0].wait()
     for k in range(chips):
         block = lax.rem(sibling + count - 2 * k, count)
@@ -312,12 +333,10 @@
     centred = feats - mean
     column = jnp.broadcast_to(jnp.sum(centred * centred, axis=0, keepdims=True), (8, channels))
     variance = group_total(column, group_width)[:1] / entries
-    normed = (centred * lax.rsqrt(variance + EPSILON) * gain_ref[...] + nbias_ref[...]).astype(BF16)
-    for load in loads[2:]:
-        load.wait()
-    queries = ((dot_n(normed, qw[...]) + qb_ref[...]) * channels ** (-0.5)).astype(BF16)
+    normed = (centred * lax.rsqrt(variance + EPSILON) * gain[...] + nbias[...]).astype(BF16)
+    queries = ((dot_n(normed, qw[...]) + qb[...]) * channels ** (-0.5)).astype(BF16)
     keys = dot_n(normed, kw[...]).astype(BF16)
-    values = (dot_n(normed, vw[...]) + vb_ref[...]).astype(BF16)
+    values = (dot_n(normed, vw[...]) + vb[...]).astype(BF16)
     scores = dot_t(queries, keys)
     query_frame = (lax.broadcasted_iota(jnp.int32, scores.shape, 0) // width) % 2
     key_frame = (lax.broadcasted_iota(jnp.int32, scores.shape, 1) // width) % 2
@@ -328,7 +347,7 @@
     denominator = jnp.sum(weights, axis=1, keepdims=True)
     attended = (dot_n(weights.astype(BF16), values) / denominator).astype(BF16)
     mixed = (
-        gath[...].reshape(tokens, channels).astype(F32) + dot_n(attended, ow[...]) + ob_ref[...]
+        gath[...].reshape(tokens, channels).astype(F32) + dot_n(attended, ow[...]) + ob[...]
     )
     mixed = mixed.astype(BF16).astype(F32).reshape(count, 2, width, channels)
     shifted_inputs(mixed[:, 0], x0_ref)
@@ -336,7 +355,7 @@
 
     outs = cw_ref.shape[1]
     lanes = 4 * outs
-    bias_row = jnp.broadcast_to(cb_ref[...], (8, channels))
+    bias_row = jnp.broadcast_to(cb[...], (8, channels))
     own = jnp.zeros((8, outs), F32)
     for k in range(count):
         own = jnp.where(me == k, bias_row[:, k * outs : (k + 1) * outs], own)
@@ -410,14 +429,15 @@
     rows = count * width
     taps = jnp.swapaxes(conv_weight, 3, 4).reshape(27, outs, channels)
     vmem = pl.BlockSpec(memory_space=pltpu.VMEM)
-    hbm = pl.BlockSpec(memory_space=pl.ANY)
+    hbm = pl.BlockSpec(memory_space=pltpu.HBM)
+    vector = pltpu.VMEM((1, channels), F32)
     square = pltpu.VMEM((channels, channels), BF16)
     row = lambda v: v.reshape(1, channels)
     out_rows = 3 * 2 * 2 * width
     decoded = pl.pallas_call(
         functools.partial(fused_kernel, count),
         out_shape=jax.ShapeDtypeStruct((out_rows, channels), BF16),
-        in_specs=[hbm, vmem, vmem, hbm, vmem, hbm, hbm, vmem, hbm, vmem, hbm, vmem],
+        in_specs=[hbm] * 12,
         out_specs=vmem,
         scratch_shapes=[
             pltpu.VMEM((count, frames * width, channels), BF16),
@@ -426,6 +446,12 @@
             square,
             square,
             pltpu.VMEM((27, outs, channels), BF16),
+            vector,
+            vector,
+            vector,
+            vector,
+            vector,
+            vector,
             pltpu.VMEM((12 * outs, 9 * channels), BF16),
             pltpu.VMEM((8 * outs, 9 * channels), BF16),
             pltpu.VMEM((rows, 9 * channels), BF16),
@@ -433,14 +459,14 @@
             pltpu.VMEM((count, 4 * width, 4 * outs), BF16),
             pltpu.VMEM((count, 4 * width, 4 * outs), BF16),
             pltpu.VMEM((channels // 128, out_rows, 128), F32),
-            pltpu.SemaphoreType.DMA((6,)),
+            pltpu.SemaphoreType.DMA((12,)),
             pltpu.SemaphoreType.DMA((count,)),
             pltpu.SemaphoreType.DMA((count,)),
             pltpu.SemaphoreType.DMA((count,)),
             pltpu.SemaphoreType.DMA((count,)),
         ],
         compiler_params=pltpu.CompilerParams(
-            collective_id=0, has_side_effects=True, vmem_limit_bytes=44 * 1024 * 1024
+            collective_id=0, has_side_effects=True, vmem_limit_bytes=63 * 1024 * 1024
         ),
     )(
         features.reshape(frames * width, channels),

time: 29.2 us -> 23.9 us (0.82)
  local copies, waits for them, and re-layouts: 7.44 us -> 1.54 us
  Pallas kernels: 21.3 us -> 22.2 us
    unnamed x25 -> x1, local copies, waits for them, and re-layouts: 7.44 us -> 1.54 us
    pallas_call x1, Pallas kernels: 21.3 us -> 22.2 us  [per_device_fused(): pl.pallas_call(functools.partial(fused_kernel, count), out_shape=jax.Shap...]
where the time goes in v2:
time: 23.9 us; the launch traced here: 23.7 us
  Pallas kernels  22.2 us (93%)
  local copies, waits for them, and re-layouts  1.54 us (6%)
    pallas_call x1, Pallas kernels, per_device_fused(): pl.pallas_call(functools.partial(fused_kernel, count), out_shape=jax.Shap...  22.2 us
    unnamed x1, local copies, waits for them, and re-layouts  1.54 us

profile of v2, /device:TPU:0, one launch (start us, length us, event | category | flops | bytes accessed | tf_op | source)
XLA Modules:
  0.0 23.7 jit_solution(2491196043263035079)
XLA Ops:
  0.0 22.2 %shard_map.118 = bf16[96,512]{1,0:T(8,128)(2,1)} custom-call(bf16[16,512]{1,0:T(8,128)(2,1)} %bitcast.13, f32[1,512]{1,0:T(1,128)} %bitcast.14, f32[1,512]{1,0:T(1,128)} %bitcast.15, bf16[512,512]{1,0:T(8,128)(2,1)} %qw_ref.1, f32[1,512]{1,0:T(1,128)} %bitcast.16, bf16[512,512]{1,0:T(8,128)(2,1)} %kw_ref.1, bf16[512,512]{1,0:T(8,128)(2,1)} %vw_ref.1, ...), custom_call_target="tpu_custom_call" | custom-call | tf_op jit(solution)/shard_map/pallas_call | solution.py:437
  22.2 1.5 %copy.14 = bf16[3,2,16,512]{3,2,1,0:T(8,128)(2,1)} copy(bf16[3,2,16,512]{3,2,1,0:T(8,128)(2,1)} %bitcast.12) | data formatting | bytes 196608

commit v3 on v2

--- a/solution.py
+++ b/solution.py
@@ -292,6 +292,7 @@
         load.start()
     pl.semaphore_wait(barrier, count - 1)
 
+    sends = []
     def feat_copy(src, block, to, slot):
         return pltpu.make_async_remote_copy(
             src_ref=src,
@@ -436,7 +437,7 @@
     out_rows = 3 * 2 * 2 * width
     decoded = pl.pallas_call(
         functools.partial(fused_kernel, count),
-        out_shape=jax.ShapeDtypeStruct((out_rows, channels), BF16),
+        out_shape=pltpu.VMEM((out_rows, channels), BF16),
         in_specs=[hbm] * 12,
         out_specs=vmem,
         scratch_shapes=[
@@ -466,21 +467,26 @@
             pltpu.SemaphoreType.DMA((count,)),
         ],
         compiler_params=pltpu.CompilerParams(
-            collective_id=0, has_side_effects=True, vmem_limit_bytes=63 * 1024 * 1024
+            collective_id=0, has_side_effects=True, vmem_limit_bytes=44 * 1024 * 1024
         ),
     )(
-        features.reshape(frames * width, channels),
-        row(norm_gain),
-        row(norm_bias),
-        query_weight,
-        row(query_bias),
-        key_weight,
-        value_weight,
-        row(value_bias),
-        out_weight,
-        row(out_bias),
-        taps,
-        row(conv_bias),
+        *(
+            pltpu.with_memory_space_constraint(operand, pltpu.HBM)
+            for operand in (
+                features.reshape(frames * width, channels),
+                row(norm_gain),
+                row(norm_bias),
+                query_weight,
+                row(query_bias),
+                key_weight,
+                value_weight,
+                row(value_bias),
+                out_weight,
+                row(out_bias),
+                taps,
+                row(conv_bias),
+            )
+        )
     )
     return decoded.reshape(3, 2, 2 * width, channels)
 

time: 23.9 us -> 22.3 us (0.933)
  local copies, waits for them, and re-layouts: 1.54 us -> 0.64 us
  Pallas kernels: 22.2 us -> 21.6 us
    unnamed x1, local copies, waits for them, and re-layouts: 1.54 us -> 0.64 us
    pallas_call x1, Pallas kernels: 22.2 us -> 21.6 us  [per_device_fused(): pl.pallas_call(functools.partial(fused_kernel, count), out_shape=pltpu.VM...]
where the time goes in v3:
time: 22.3 us; the launch traced here: 22.2 us
  Pallas kernels  21.6 us (97%)
  local copies, waits for them, and re-layouts  0.64 us (3%)
    pallas_call x1, Pallas kernels, per_device_fused(): pl.pallas_call(functools.partial(fused_kernel, count), out_shape=pltpu.VM...  21.6 us
    unnamed x1, local copies, waits for them, and re-layouts  0.64 us

profile of v3, /device:TPU:0, one launch (start us, length us, event | category | flops | bytes accessed | tf_op | source)
XLA Modules:
  0.0 22.2 jit_solution(10547287021660590806)
XLA Ops:
  0.0 21.6 %shard_map.118 = bf16[96,512]{1,0:T(8,128)(2,1)S(1)} custom-call(bf16[16,512]{1,0:T(8,128)(2,1)} %bitcast.13, f32[1,512]{1,0:T(1,128)} %bitcast.14, f32[1,512]{1,0:T(1,128)} %bitcast.15, bf16[512,512]{1,0:T(8,128)(2,1)} %qw_ref.1, f32[1,512]{1,0:T(1,128)} %bitcast.16, bf16[512,512]{1,0:T(8,128)(2,1)} %kw_ref.1, bf16[512,512]{1,0:T(8,128)(2,1)} %vw_ref.1, ...), custom_call_target="tpu_custom_call" | custom-call | tf_op jit(solution)/shard_map/pallas_call | solution.py:438
  21.6 0.6 %copy.14 = bf16[3,2,16,512]{3,2,1,0:T(8,128)(2,1)} copy(bf16[3,2,16,512]{3,2,1,0:T(8,128)(2,1)S(1)} %bitcast.11) | data formatting | bytes 196608

commit v4 on v3

--- a/solution.py
+++ b/solution.py
@@ -389,14 +389,22 @@
         sends.append(send)
     own_copy = pltpu.make_async_copy(sendbuf.at[me], recvbuf.at[me], osend_sem.at[0])
     own_copy.start()
-    own_copy.wait()
-    for k in range(1, count):
-        source = lax.rem(me + count - k, count)
-        out_copy(source, source, me, k).wait_recv()
 
     each = 128 // outs
-    for j in range(count // each):
-        parts = [recvbuf[j * each + i].astype(F32) for i in range(each)]
+    blocks = count // each
+    for step in range(blocks):
+        j = lax.rem(me // each + step, blocks)
+        first_source = j * each
+        if step == 0:
+            own_copy.wait()
+            for m in range(1, each):
+                source = first_source + lax.rem(me + m, each)
+                out_copy(source, source, me, m).wait_recv()
+        else:
+            for m in range(each):
+                source = first_source + m
+                out_copy(source, source, me, 1).wait_recv()
+        parts = [recvbuf[first_source + i].astype(F32) for i in range(each)]
         for p in range(2):
             for q in range(2):
                 at = (p * 2 + q) * outs

time: 22.3 us -> 22.3 us (level)
  no operation moved by 1% of the time
where the time goes in v4:
time: 22.3 us; the launch traced here: 22.1 us
  Pallas kernels  21.5 us (96%)
  local copies, waits for them, and re-layouts  0.64 us (3%)
    pallas_call x1, Pallas kernels, per_device_fused(): pl.pallas_call(functools.partial(fused_kernel, count), out_shape=pltpu.VM...  21.5 us
    unnamed x1, local copies, waits for them, and re-layouts  0.64 us

profile of v4, /device:TPU:0, one launch (start us, length us, event | category | flops | bytes accessed | tf_op | source)
XLA Modules:
  0.0 22.1 jit_solution(4622208369059332566)
XLA Ops:
  0.0 21.5 %shard_map.118 = bf16[96,512]{1,0:T(8,128)(2,1)S(1)} custom-call(bf16[16,512]{1,0:T(8,128)(2,1)} %bitcast.13, f32[1,512]{1,0:T(1,128)} %bitcast.14, f32[1,512]{1,0:T(1,128)} %bitcast.15, bf16[512,512]{1,0:T(8,128)(2,1)} %qw_ref.1, f32[1,512]{1,0:T(1,128)} %bitcast.16, bf16[512,512]{1,0:T(8,128)(2,1)} %kw_ref.1, bf16[512,512]{1,0:T(8,128)(2,1)} %vw_ref.1, ...), custom_call_target="tpu_custom_call" | custom-call | tf_op jit(solution)/shard_map/pallas_call | solution.py:446
  21.5 0.6 %copy.14 = bf16[3,2,16,512]{3,2,1,0:T(8,128)(2,1)} copy(bf16[3,2,16,512]{3,2,1,0:T(8,128)(2,1)S(1)} %bitcast.11) | data formatting | bytes 196608
